TPU v7x, 32 devices: a whole 2x2x4 slice. The times are simulated.
32 devices in a mesh: dp: 8 (over z, y), sp: 4 (over x, core).
Axes of the slice: x: 2, y: 2, z: 4, core: 2. Of those that a mesh axis runs over, the one named last changes fastest.
Arguments:
- clip_input: float32 [256, 4, 8, 7, 512], P('dp', None, 'sp'), may hold values from -6 to 6
- space_weight: bfloat16 [3, 3, 512, 1152], replicated, may hold values from -0.09375 to 0.09375
- time_weight: bfloat16 [3, 1152, 512], replicated, may hold values from -0.109375 to 0.109375
- gain_mid: float32 [1152], replicated, may hold values from 0.5 to 1.5
- shift_mid: float32 [1152], replicated, may hold values from -1.5 to 1.5
- gain_out: float32 [512], replicated, may hold values from 0.5 to 1.5
- shift_out: float32 [512], replicated, may hold values from -1.5 to 1.5
- class_weight: float32 [512, 400], replicated, may hold values from -0.25 to 0.25
- class_bias: float32 [400], replicated, may hold values from -2.5 to 2.5
- frames: int32 [256], P('dp'), may hold values from 1 to 4, as said below
- rows: int32 [256], P('dp'), may hold values from 1 to 8, as said below
- cols: int32 [256], P('dp'), may hold values from 1 to 7
- logit_grad: float32 [256, 400], P('dp'), may hold values from -6 to 6
Outputs:
- logits: float32 [256, 400], P('dp')
- input_grad: float32 [256, 4, 8, 7, 512], P('dp', None, 'sp')
- space_grad: float32 [3, 3, 512, 1152], replicated
- time_grad: float32 [3, 1152, 512], replicated
- gain_mid_grad: float32 [1152], replicated
- shift_mid_grad: float32 [1152], replicated
- gain_out_grad: float32 [512], replicated
- shift_out_grad: float32 [512], replicated
- class_weight_grad: float32 [512, 400], replicated
- class_bias_grad: float32 [400], replicated
Inputs may be any that keep to these rules, and one draw needn't show every extreme that they name: `frames`: each value is 1, 2 or 4; both 1 and 4 occur. In each aligned block of 32 clips one clip has all 8 rows; some clip has 1 row.
All inputs are finite; a program needn't handle non-finite values.
Results may differ from a plain program's by a relative error of at most 0.0065.
Values may be sent and summed in bfloat16 or wider, within the bound.
No kernel may reach another device: no remote copies, remote signals or barrier semaphores. Data moves between devices by JAX's collectives and lax.ppermute only.
A program may use at most 192 MiB of HBM per device.

v0:
```python
import math

import jax
import jax.numpy as jnp
from jax import lax
from jax.sharding import PartitionSpec as P

EPSILON = 1e-05
HIGH = lax.Precision.HIGHEST


def extended(block, sides, width):
    for axis, dim in sides:
        count = lax.axis_size(axis)
        forward = [(i, i + 1) for i in range(count - 1)]
        backward = [(target, source) for source, target in forward]
        low = lax.ppermute(
            lax.slice_in_dim(block, block.shape[dim] - width, None, axis=dim), axis, forward
        )
        high = lax.ppermute(lax.slice_in_dim(block, 0, width, axis=dim), axis, backward)
        block = jnp.concatenate([low, block, high], axis=dim)
    return block


def silu_slope(values):
    sigma = jax.nn.sigmoid(values)
    return sigma * (1.0 + values * (1.0 - sigma))


def valid_mask(frames, rows, cols, frame_count, row_count, col_count):
    row_start = lax.axis_index("sp") * row_count
    frame_ok = jnp.arange(frame_count)[None, :] < frames[:, None]
    row_ok = (row_start + jnp.arange(row_count))[None, :] < rows[:, None]
    col_ok = jnp.arange(col_count)[None, :] < cols[:, None]
    joined = frame_ok[:, :, None, None] & row_ok[:, None, :, None] & col_ok[:, None, None, :]
    return joined.astype(jnp.float32)[..., None]


def space_conv(padded, weight, row_count, col_count):
    total = None
    for row_off in range(3):
        for col_off in range(3):
            term = jnp.einsum(
                "bthwc,cm->bthwm",
                padded[:, :, row_off : row_off + row_count, col_off : col_off + col_count, :],
                weight[row_off, col_off],
                preferred_element_type=jnp.float32,
            )
            total = term if total is None else total + term
    return total


def norm_stats(values, mask):
    local_count = jnp.sum(mask)
    count_all, total = lax.psum(
        (local_count, jnp.sum(values * mask, axis=(0, 1, 2, 3))), ("dp", "sp")
    )
    center = total / count_all
    offset = values - center
    spread = lax.psum(jnp.sum(mask * offset * offset, axis=(0, 1, 2, 3)), ("dp", "sp")) / count_all
    return (center, lax.rsqrt(spread + EPSILON), count_all)


def norm_back(grad_out, normed, gain, scale, mask, count_all):
    shift_grad, gain_grad = lax.psum(
        (jnp.sum(grad_out, axis=(0, 1, 2, 3)), jnp.sum(grad_out * normed, axis=(0, 1, 2, 3))),
        ("dp", "sp"),
    )
    grad_in = gain * scale * (grad_out - mask * (shift_grad + normed * gain_grad) / count_all)
    return (grad_in, gain_grad, shift_grad)


def pack_flat(arrays):
    flat = jnp.concatenate([item.reshape(-1) for item in arrays])
    length = flat.shape[0]
    groups = lax.axis_size(("dp", "sp"))
    lines = -(-length // 128)
    lines = -(-lines // groups) * groups
    return flat.reshape(lines, 128)


def unpack_flat(whole, shapes):
    flat = whole.reshape(-1)
    pieces = []
    offset = 0
    for dims in shapes:
        length = math.prod(dims)
        pieces.append(flat[offset : offset + length].reshape(dims))
        offset += length
    return pieces


def shards(
    clip_input,
    space_weight,
    time_weight,
    gain_mid,
    shift_mid,
    gain_out,
    shift_out,
    class_weight,
    class_bias,
    frames,
    rows,
    cols,
    logit_grad,
):
    clip_count, frame_count, row_count, col_count, width = clip_input.shape
    mask = valid_mask(frames, rows, cols, frame_count, row_count, col_count)
    masked_input = clip_input * mask
    input_low = masked_input.astype(jnp.bfloat16)
    with_rim = extended(input_low, (("sp", 2),), 1)
    padded_input = jnp.pad(with_rim, ((0, 0), (0, 0), (0, 0), (1, 1), (0, 0)))
    mid_pre = space_conv(padded_input, space_weight, row_count, col_count)
    mid_center, mid_scale, count_all = norm_stats(mid_pre, mask)
    mid_normed = (mid_pre - mid_center) * mid_scale
    mid_act = gain_mid * mid_normed + shift_mid
    mid_low = (jax.nn.silu(mid_act) * mask).astype(jnp.bfloat16)
    mid_padded = jnp.pad(mid_low, ((0, 0), (1, 1), (0, 0), (0, 0), (0, 0)))
    out_pre = None
    for offset in range(3):
        term = jnp.einsum(
            "bthwm,mc->bthwc",
            mid_padded[:, offset : offset + frame_count],
            time_weight[offset],
            preferred_element_type=jnp.float32,
        )
        out_pre = term if out_pre is None else out_pre + term
    out_center, out_scale, second_count = norm_stats(out_pre, mask)
    out_normed = (out_pre - out_center) * out_scale
    out_act = gain_out * out_normed + shift_out + masked_input
    block_out = jax.nn.silu(out_act) * mask
    clip_cells = (frames * rows * cols).astype(jnp.float32)
    pooled = lax.psum(jnp.sum(block_out, axis=(1, 2, 3)), "sp") / clip_cells[:, None]
    logits = jnp.dot(pooled, class_weight, precision=HIGH) + class_bias
    class_weight_grad, class_bias_grad = lax.psum(
        (jnp.dot(pooled.T, logit_grad, precision=HIGH), jnp.sum(logit_grad, axis=0)), "dp"
    )
    pooled_grad = jnp.dot(logit_grad, class_weight.T, precision=HIGH) / clip_cells[:, None]
    act_grad = pooled_grad[:, None, None, None, :] * mask * silu_slope(out_act)
    out_grad, gain_out_grad, shift_out_grad = norm_back(
        act_grad, out_normed, gain_out, out_scale, mask, second_count
    )
    out_grad_low = out_grad.astype(jnp.bfloat16)
    time_grad = jnp.stack(
        [
            jnp.einsum(
                "bthwm,bthwc->mc",
                mid_padded[:, offset : offset + frame_count],
                out_grad_low,
                preferred_element_type=jnp.float32,
            )
            for offset in range(3)
        ]
    )
    grad_padded = jnp.pad(out_grad_low, ((0, 0), (1, 1), (0, 0), (0, 0), (0, 0)))
    mid_back = None
    for offset in range(3):
        term = jnp.einsum(
            "bthwc,mc->bthwm",
            grad_padded[:, 2 - offset : 2 - offset + frame_count],
            time_weight[offset],
            preferred_element_type=jnp.float32,
        )
        mid_back = term if mid_back is None else mid_back + term
    mid_again = space_conv(padded_input, space_weight, row_count, col_count)
    normed_back = (mid_again - mid_center) * mid_scale
    mid_act_grad = mid_back * mask * silu_slope(gain_mid * normed_back + shift_mid)
    mid_grad, gain_mid_grad, shift_mid_grad = norm_back(
        mid_act_grad, normed_back, gain_mid, mid_scale, mask, count_all
    )
    mid_grad_low = mid_grad.astype(jnp.bfloat16)
    space_grad = jnp.stack(
        [
            jnp.stack(
                [
                    jnp.einsum(
                        "bthwc,bthwm->cm",
                        padded_input[
                            :, :, row_off : row_off + row_count, col_off : col_off + col_count, :
                        ],
                        mid_grad_low,
                        preferred_element_type=jnp.float32,
                    )
                    for col_off in range(3)
                ]
            )
            for row_off in range(3)
        ]
    )
    grad_rim = extended(mid_grad_low, (("sp", 2),), 1)
    grad_wide = jnp.pad(grad_rim, ((0, 0), (0, 0), (0, 0), (1, 1), (0, 0)))
    input_back = None
    for row_off in range(3):
        for col_off in range(3):
            term = jnp.einsum(
                "bthwm,cm->bthwc",
                grad_wide[
                    :,
                    :,
                    2 - row_off : 2 - row_off + row_count,
                    2 - col_off : 2 - col_off + col_count,
                    :,
                ],
                space_weight[row_off, col_off],
                preferred_element_type=jnp.float32,
            )
            input_back = term if input_back is None else input_back + term
    input_grad = (input_back + act_grad) * mask
    both_share = lax.psum_scatter(
        pack_flat([space_grad, time_grad]), ("dp", "sp"), scatter_dimension=0, tiled=True
    )
    space_grad, time_grad = unpack_flat(
        lax.all_gather(both_share, ("dp", "sp"), axis=0, tiled=True),
        [space_grad.shape, time_grad.shape],
    )
    return (
        logits,
        input_grad,
        space_grad,
        time_grad,
        gain_mid_grad,
        shift_mid_grad,
        gain_out_grad,
        shift_out_grad,
        class_weight_grad,
        class_bias_grad,
    )


def solution(mesh):
    placed = (
        P("dp", None, "sp", None, None),
        P(),
        P(),
        P(),
        P(),
        P(),
        P(),
        P(),
        P(),
        P("dp"),
        P("dp"),
        P("dp"),
        P("dp", None),
    )
    return jax.shard_map(
        shards,
        mesh=mesh,
        in_specs=placed,
        out_specs=(
            P("dp", None),
            P("dp", None, "sp", None, None),
            P(),
            P(),
            P(),
            P(),
            P(),
            P(),
            P(),
            P(),
        ),
        check_vma=False,
    )
```

profile of v0, /device:TPU:0, one launch (start us, length us, event | category | flops | bytes accessed | tf_op | source)
XLA Modules:
  0.0 1024.8 jit_solution(7833674470203486645)
XLA Ops:
  20.8 7.2 fusion.66
  68.7 26.2 %multiply_reduce_fusion.1 = (f32[1152]{0:T(1024)S(1)}, f32[32,4,2,7,1152]{4,0,3,2,1:T(8,128)}) fusion(f32[32,4,2,7]{0,3,2,1:T(8,128)S(1)} %and_convert_fusion, bf16[3,3,512,1152]{3,2,1,0:T(8,128)(2,1)} %param.14, bf16[32,4,1,7,512]{4,0,3,2,1:T(8,128)(2,1)} %copy-done.1, bf16[32,4,2,7,512]{4,0,3,2,1:T(8,128)(2,1)S(1)} %fusion.25, ...), kind=kOutput, calls=%fused_computation.11 | convolution fusion | flops 1843592064 | bytes 79179264 | tf_op jit(solution)/shard_map/bthwc,cm->bthwm/dot_general | solution.py:43
  94.9 42.2 %all-reduce.6 = (f32[1152]{0:T(1024)S(1)}, f32[]{:T(128)}) all-reduce(f32[1152]{0:T(1024)S(1)} %get-tuple-element.60, f32[]{:T(128)} %convert_reduce_fusion), channel_id=1, replica_groups=mesh['dp'=8,'sp'=4] {'dp','sp'}, use_global_device_ids=true, to_apply=%region_1.2 | all-reduce | flops 1153 | bytes 9224 | tf_op jit(solution)/shard_map/psum | solution.py:55
  141.9 40.8 %psum.89 = f32[1152]{0:T(1024)S(1)} all-reduce(f32[1152]{0:T(1024)S(1)} %fusion), channel_id=1, replica_groups=mesh['dp'=8,'sp'=4] {'dp','sp'}, use_global_device_ids=true, to_apply=%region_5.6 | all-reduce | flops 1152 | bytes 9216 | tf_op jit(solution)/shard_map/psum | solution.py:60
  198.4 39.8 %psum.90 = f32[512]{0:T(512)S(1)} all-reduce(f32[512]{0:T(512)S(1)} %get-tuple-element.62), channel_id=1, replica_groups=mesh['dp'=8,'sp'=4] {'dp','sp'}, use_global_device_ids=true, to_apply=%region_7.8 | all-reduce | flops 512 | bytes 4096 | tf_op jit(solution)/shard_map/psum | solution.py:55
  241.5 40.2 %psum.91 = f32[512]{0:T(512)S(1)} all-reduce(f32[512]{0:T(512)S(1)} %fusion.15), channel_id=1, replica_groups=mesh['dp'=8,'sp'=4] {'dp','sp'}, use_global_device_ids=true, to_apply=%region_9.10 | all-reduce | flops 512 | bytes 4096 | tf_op jit(solution)/shard_map/psum | solution.py:60
  282.4 7.6 multiply_reduce_fusion.2
  290.0 39.9 %all-reduce.5 = (f32[512]{0:T(512)S(1)}, f32[512]{0:T(512)S(1)}) all-reduce(f32[512]{0:T(512)S(1)} %get-tuple-element.32, f32[512]{0:T(512)S(1)} %get-tuple-element.34), channel_id=1, replica_groups=mesh['dp'=8,'sp'=4] {'dp','sp'}, use_global_device_ids=true, to_apply=%region_15.16 | all-reduce | flops 1024 | bytes 8192 | tf_op jit(solution)/shard_map/psum | solution.py:65
  368.0 12.3 %fusion.130 = (f32[1152]{0:T(1024)S(1)}, f32[1152]{0:T(1024)S(1)}, f32[32,4,2,7,1152]{4,0,3,2,1:T(8,128)}) fusion(f32[1152]{0:T(1024)S(1)} %get-tuple-element.42, f32[32,4,2,7,1152]{4,0,3,2,1:T(8,128)S(1)} %bitcast.215, f32[1152]{0:T(1024)S(1)} %broadcast_divide_fusion.3, f32[1152]{0:T(1024)S(1)} %copy-done.24, f32[1152]{0:T(1024)S(1)} %copy-done.21, ...), kind=kOutput, calls=%fused_computation.184 | convolution fusion | flops 1622603520 | bytes 36079616 | tf_op jit(solution)/shard_map/bthwc,mc->bthwm/dot_general | solution.py:159
  380.3 40.3 %all-reduce.4 = (f32[1152]{0:T(1024)S(1)}, f32[1152]{0:T(1024)S(1)}) all-reduce(f32[1152]{0:T(1024)S(1)} %get-tuple-element.31, f32[1152]{0:T(1024)S(1)} %get-tuple-element.30), channel_id=1, replica_groups=mesh['dp'=8,'sp'=4] {'dp','sp'}, use_global_device_ids=true, to_apply=%region_19.20 | all-reduce | flops 2304 | bytes 18432 | tf_op jit(solution)/shard_map/psum | solution.py:65
  420.6 7.9 multiply_convert_fusion
  463.8 7.6 pad_maximum_fusion
  471.4 21.9 %reshape.137 = f32[5308416]{0:T(1024)} reshape(f32[3,3,512,1152]{3,2,1,0:T(8,128)} %pad_maximum_fusion) | data formatting | bytes 42467328 | tf_op jit(solution)/shard_map/reshape | solution.py:74
  493.3 24.6 %maximum_bitcast_fusion = f32[55296,128]{1,0:T(8,128)} fusion(f32[1769472]{0:T(1024)} %bitcast.216, f32[5308416]{0:T(1024)} %reshape.137), kind=kLoop, calls=%fused_computation | loop fusion | flops 7077888 | bytes 56623104 | tf_op jit(solution)/shard_map/reshape | solution.py:79
  518.6 263.8 %reduce-scatter.2.cloned.1.call-done = f32[1728,128]{1,0:T(8,128)} async-done(((f32[55296,128]{1,0:T(8,128)}), f32[1728,128]{1,0:T(8,128)}) %reduce-scatter.2.cloned.1.call-update) | async-done | bytes 884752 | tf_op jit(solution)/shard_map/reduce_scatter | solution.py:210
  791.2 21.5 %psum.98 = f32[400]{0:T(512)} all-reduce(f32[400]{0:T(512)S(1)} %reduce_sum.113), channel_id=1, replica_groups=mesh['dp'=8,'sp'=4] {'dp'}, use_global_device_ids=true, to_apply=%region_23.24 | all-reduce | flops 400 | bytes 3200 | tf_op jit(solution)/shard_map/psum | solution.py:136
  812.7 7.0 fusion.64
  824.8 7.3 fusion.5
  832.0 7.0 fusion.56
  869.0 18.8 %add_multiply_fusion = f32[32,4,2,7,512]{4,0,3,2,1:T(8,128)} fusion(f32[32,4,2,7,512]{4,0,3,2,1:T(8,128)} %get-tuple-element.45, f32[32,4,2,7,512]{4,0,3,2,1:T(8,128)} %fusion.5, f32[32,4,2,7,512]{4,0,3,2,1:T(8,128)} %fusion.56, f32[32,4,2,7,512]{4,0,3,2,1:T(8,128)} %fusion.60, f32[32,4,2,7,512]{4,0,3,2,1:T(8,128)} %fusion.64, ...), kind=kOutput, calls=%fused_computation.44 | convolution fusion | flops 1845886976 | bytes 46144512 | tf_op jit(solution)/shard_map/bthwm,cm->bthwc/dot_general | solution.py:196
  894.6 68.6 %all-gather.2.cloned.1.call-done = f32[55296,128]{1,0:T(8,128)} async-done(((f32[1728,128]{1,0:T(8,128)}), f32[55296,128]{1,0:T(8,128)}) %all-gather.2.cloned.1.call-update) | async-done | bytes 28311568 | tf_op jit(solution)/shard_map/all_gather | solution.py:214
  963.2 15.1 %slice.214 = f32[41472,128]{1,0:T(8,128)} slice(f32[55296,128]{1,0:T(8,128)} %all-gather.2.cloned.1.call-done), slice={[0:41472], [0:128]} | slice | bytes 42467328 | tf_op jit(solution)/shard_map/slice | solution.py:88
  978.3 23.1 %reshape.140 = f32[3,3,512,1152]{3,2,1,0:T(8,128)} reshape(f32[41472,128]{1,0:T(8,128)} %slice.214) | data formatting | bytes 42467328 | tf_op jit(solution)/shard_map/reshape | solution.py:88
  1006.4 8.6 reshape.141
  (175 shorter events, 209.3 us)
Async XLA Ops:
  8.0 12.2 %copy-start = (f32[512,400]{0,1:T(8,128)S(1)}, f32[512,400]{0,1:T(8,128)}, u32[]{:S(2)}) copy-start(f32[512,400]{0,1:T(8,128)} %param.20) | copy-start | bytes 2457604
  8.0 774.3 %reduce-scatter.2.cloned.1.call-start = ((), (), s32[]{:S(2)}) async-start(), calls=%async_computation.2 | async-start | bytes 29196288 | tf_op jit(solution)/shard_map/reduce_scatter | solution.py:210
  10.2 9.3 copy-start.33
  10.3 10.0 copy-start.19
  10.3 17.7 %slice-start.2 = ((s8[10616832]{0:T(1024)(128)(4,1)}), s8[4194304]{0:T(1024)(128)(4,1)S(1)}, s32[]{:S(2)}) async-start(s8[10616832]{0:T(1024)(128)(4,1)} %bitcast.218), calls=%async_computation.7 | async-start | bytes 8388608
  14.6 13.4 %slice-start.3 = ((s8[10616832]{0:T(1024)(128)(4,1)}), s8[4194304]{0:T(1024)(128)(4,1)S(1)}, s32[]{:S(2)}) async-start(s8[10616832]{0:T(1024)(128)(4,1)} %bitcast.218), calls=%async_computation.8 | async-start | bytes 8388608
  14.7 13.3 %collective-permute-start.1 = (bf16[32,4,1,7,512]{4,0,3,2,1:T(8,128)(2,1)S(1)}, bf16[32,4,1,7,512]{4,0,3,2,1:T(8,128)(2,1)S(1)}, u32[]{:S(2)}, u32[]{:S(2)}) collective-permute-start(bf16[32,4,1,7,512]{4,0,3,2,1:T(8,128)(2,1)S(1)} %get-tuple-element.59), channel_id=1, source_target_pairs={{1,0},{2,1},{3,2},{5,4},{6,5},{7,6},{9,8},{10,9},{11,10},{13,12},{... | collective-permute-start | bytes 2752520 | tf_op jit(solution)/shard_map/ppermute | solution.py:20
  16.3 17.7 %collective-permute-start = (bf16[32,4,1,7,512]{4,0,3,2,1:T(8,128)(2,1)S(1)}, bf16[32,4,1,7,512]{4,0,3,2,1:T(8,128)(2,1)S(1)}, u32[]{:S(2)}, u32[]{:S(2)}) collective-permute-start(bf16[32,4,1,7,512]{4,0,3,2,1:T(8,128)(2,1)S(1)} %get-tuple-element.58), channel_id=1, source_target_pairs={{0,1},{1,2},{2,3},{4,5},{5,6},{6,7},{8,9},{9,10},{10,11},{12,13},{... | collective-permute-start | bytes 2752520 | tf_op jit(solution)/shard_map/ppermute | solution.py:17
  28.0 29.2 %copy-start.1 = (bf16[32,4,1,7,512]{4,0,3,2,1:T(8,128)(2,1)}, bf16[32,4,1,7,512]{4,0,3,2,1:T(8,128)(2,1)S(1)}, u32[]{:S(2)}) copy-start(bf16[32,4,1,7,512]{4,0,3,2,1:T(8,128)(2,1)S(1)} %collective-permute-done.1) | copy-start | bytes 2752516
  33.9 29.1 %copy-start.4 = (bf16[32,4,1,7,512]{4,0,3,2,1:T(8,128)(2,1)}, bf16[32,4,1,7,512]{4,0,3,2,1:T(8,128)(2,1)S(1)}, u32[]{:S(2)}) copy-start(bf16[32,4,1,7,512]{4,0,3,2,1:T(8,128)(2,1)S(1)} %collective-permute-done) | copy-start | bytes 2752516
  137.8 44.9 %copy-start.21 = (f32[1152]{0:T(1024)S(1)}, f32[1152]{0:T(1024)}, u32[]{:S(2)}) copy-start(f32[1152]{0:T(1024)} %param.16) | copy-start | bytes 13828
  137.8 45.5 %copy-start.24 = (f32[1152]{0:T(1024)S(1)}, f32[1152]{0:T(1024)}, u32[]{:S(2)}) copy-start(f32[1152]{0:T(1024)} %param.17) | copy-start | bytes 13828
  193.8 87.9 %copy-start.27 = (f32[512]{0:T(512)S(1)}, f32[512]{0:T(512)}, u32[]{:S(2)}) copy-start(f32[512]{0:T(512)} %param.18) | copy-start | bytes 6148
  193.8 88.6 %copy-start.28 = (f32[512]{0:T(512)S(1)}, f32[512]{0:T(512)}, u32[]{:S(2)}) copy-start(f32[512]{0:T(512)} %param.19) | copy-start | bytes 6148
  334.6 17.5 %copy-start.17 = (bf16[32,4,2,7,512]{4,0,3,2,1:T(8,128)(2,1)}, bf16[32,4,2,7,512]{4,0,3,2,1:T(8,128)(2,1)S(1)}, u32[]{:S(2)}) copy-start(bf16[32,4,2,7,512]{4,0,3,2,1:T(8,128)(2,1)S(1)} %multiply_convert_fusion.2) | copy-start | bytes 5505028
  428.4 26.5 %copy-start.7 = (bf16[32,4,2,7,1152]{4,0,3,2,1:T(8,128)(2,1)}, bf16[32,4,2,7,1152]{4,0,3,2,1:T(8,128)(2,1)S(1)}, u32[]{:S(2)}) copy-start(bf16[32,4,2,7,1152]{4,0,3,2,1:T(8,128)(2,1)S(1)} %multiply_convert_fusion) | copy-start | bytes 12386308
  517.9 301.8 %all-reduce.10.cloned.1.call-start = ((), (), s32[]{:S(2)}) async-start(), calls=%async_computation.1 | async-start | bytes 131072 | tf_op jit(solution)/shard_map/psum | solution.py:134
  518.5 444.7 %all-gather.2.cloned.1.call-start = ((), (), s32[]{:S(2)}) async-start(), calls=%async_computation.3 | async-start | bytes 29196288 | tf_op jit(solution)/shard_map/all_gather | solution.py:214
  782.4 232.6 %all-reduce.12.cloned.1.call-start = ((), (), s32[]{:S(2)}) async-start(), calls=%async_computation.4 | async-start | bytes 1638400 | tf_op jit(solution)/shard_map/psum | solution.py:136
  787.0 37.7 %collective-permute-start.2 = (bf16[32,4,1,7,1152]{4,0,3,2,1:T(8,128)(2,1)}, bf16[32,4,1,7,1152]{4,0,3,2,1:T(8,128)(2,1)}, u32[]{:S(2)}, u32[]{:S(2)}) collective-permute-start(bf16[32,4,1,7,1152]{4,0,3,2,1:T(8,128)(2,1)} %get-tuple-element.49), channel_id=1, source_target_pairs={{0,1},{1,2},{2,3},{4,5},{5,6},{6,7},{8,9},{9,10},{10,11},{12,13},{... | collective-permute-start | bytes 6193160 | tf_op jit(solution)/shard_map/ppermute | solution.py:17
  789.9 42.1 %collective-permute-start.3 = (bf16[32,4,1,7,1152]{4,0,3,2,1:T(8,128)(2,1)}, bf16[32,4,1,7,1152]{4,0,3,2,1:T(8,128)(2,1)}, u32[]{:S(2)}, u32[]{:S(2)}) collective-permute-start(bf16[32,4,1,7,1152]{4,0,3,2,1:T(8,128)(2,1)} %get-tuple-element.48), channel_id=1, source_target_pairs={{1,0},{2,1},{3,2},{5,4},{6,5},{7,6},{9,8},{10,9},{11,10},{13,12},{... | collective-permute-start | bytes 6193160 | tf_op jit(solution)/shard_map/ppermute | solution.py:20
  812.7 9.6 copy-start.29
  824.7 14.3 %slice-start.5 = ((s8[10616832]{0:T(1024)(128)(4,1)}), s8[4194304]{0:T(1024)(128)(4,1)S(1)}, s32[]{:S(2)}) async-start(s8[10616832]{0:T(1024)(128)(4,1)} %bitcast.220), calls=%async_computation.10 | async-start | bytes 8388608
  824.7 14.3 %slice-start.6 = ((s8[10616832]{0:T(1024)(128)(4,1)}), s8[4194304]{0:T(1024)(128)(4,1)S(1)}, s32[]{:S(2)}) async-start(s8[10616832]{0:T(1024)(128)(4,1)} %bitcast.220), calls=%async_computation.11 | async-start | bytes 8388608
  (29 other events, 166.0 us)
Sparse Core Ops, SparseCore 0:
  518.1 264.2 reduce-scatter.1
  785.7 177.4 all-gather.1
Sparse Core Ops, SparseCore 1:
  521.3 31.4 all-reduce.9
  822.5 164.4 all-reduce.11
where the time goes:
time: 1030 us; the launch traced here: 1020 us
  waiting for transfers between devices  333 us (32%)
  blocking collectives  265 us (26%)
  matrix products  220 us (21%)
  local copies, waits for them, and re-layouts  101 us (10%)
  other arithmetic  80.4 us (8%)
  between operations  16.4 us (2%)
    reduce_scatter x1, waiting for transfers between devices, shards(): lax.psum_scatter(pack_flat([space_grad, time_grad]), ('dp', 'sp'), scatte...  264 us
    psum x2, blocking collectives, norm_stats(): lax.psum((local_count, jnp.sum(values * mask, axis=(0, 1, 2, 3))), ('dp',...  82 us
    psum x2, blocking collectives, norm_stats(): lax.psum(jnp.sum(mask * offset * offset, axis=(0, 1, 2, 3)), ('dp', 'sp'))  81 us
    psum x2, blocking collectives, norm_back(): lax.psum((jnp.sum(grad_out, axis=(0, 1, 2, 3)), jnp.sum(grad_out * normed...  80.1 us
    dot_general x9, matrix products, space_conv(): jnp.einsum('bthwc,cm->bthwm', padded[:, :, row_off:row_off + row_count, c...  74 us
    dot_general x9, matrix products, shards(): jnp.einsum('bthwm,cm->bthwc', grad_wide[:, :, 2 - row_off:2 - row_off + r...  70 us
    all_gather x1, waiting for transfers between devices, shards(): lax.all_gather(both_share, ('dp', 'sp'), axis=0, tiled=True)  68.6 us
    reshape x2, local copies, waits for them, and re-layouts, unpack_flat(): pieces.append(flat[offset:offset + length].reshape(dims))  31.7 us
  transfers between devices with their start and end apart: 8, of which 2 were waited for; matrix products, arithmetic and copies ran while one was open for 15% of the time, Pallas kernels for 0%

commit v1 on v0

v1 whole, which is shorter than its diff:
```python
import functools

import jax
import jax.numpy as jnp
from jax import lax
from jax.experimental import pallas as pl
from jax.experimental.pallas import tpu as pltpu
from jax.sharding import PartitionSpec as P

EPSILON = 1e-05
HIGH = lax.Precision.HIGHEST
F32 = jnp.float32
BF16 = jnp.bfloat16
S_AT, BLOCKS_AT, CORE_AT, ROW_AT, OFF, LEN, PAD, END_AT = 0, 1, 2, 3, 4, 8, 12, 16

VM = pl.BlockSpec(memory_space=pltpu.VMEM)
SM = pl.BlockSpec(memory_space=pltpu.SMEM)
ANY = pl.BlockSpec(memory_space=pl.ANY)


def params(mib):
    return pltpu.CompilerParams(vmem_limit_bytes=mib << 20)


def nt_dot(a, b):
    return lax.dot_general(a, b, (((1,), (1,)), ((), ())), preferred_element_type=F32)


def tn_dot(a, b):
    return lax.dot_general(a, b, (((0,), (0,)), ((), ())), preferred_element_type=F32)


def dot(a, b):
    return jnp.dot(a, b, preferred_element_type=F32)


def split(value):
    high = value.astype(BF16)
    return high, (value - high.astype(F32)).astype(BF16)


def sigmoid(v):
    return 1.0 / (1.0 + jnp.exp(-v))


def slope(v):
    s = sigmoid(v)
    return s * (1.0 + v * (1.0 - s))


def at16(index):
    return pl.multiple_of(index, 16)


def at128(index):
    return pl.multiple_of(index, 128)


def pick_rows(row_info, shift):
    place, col, cols = row_info[0:1, :], row_info[1:2, :], row_info[2:3, :]
    home = col - shift
    ok = (col < cols) & (home >= 0) & (home < cols)
    spot = jnp.where(ok, place - shift, -1)
    size = row_info.shape[1]
    index = lax.broadcasted_iota(jnp.int32, (size, size), 0)
    return jnp.where(index == spot, 1.0, 0.0).astype(BF16)


def pick_cols(col_info, shift):
    place, col, cols = col_info[:, 0:1], col_info[:, 1:2], col_info[:, 2:3]
    home = col - shift
    ok = (col < cols) & (home >= 0) & (home < cols)
    spot = jnp.where(ok, place - shift, -1)
    size = col_info.shape[0]
    index = lax.broadcasted_iota(jnp.int32, (size, size), 1)
    return jnp.where(index == spot, 1.0, 0.0).astype(BF16)


def each_list(meta, base, frame_count, store):
    for t in range(frame_count):
        for half in range(2):

            @pl.when(half * 128 < meta[PAD + t])
            def _(t=t, half=half):
                store(t, half, at16(base + meta[OFF + t] + half * 128))


def space_kernel(
    meta, row_info, own, part, outer, weight, mid_pre, belong, stats, planes, packed, kernel, pick, sems
):
    frame_count = own.shape[1]
    core = meta[CORE_AT]
    s = meta[S_AT]
    copies = [
        pltpu.make_async_copy(weight, kernel, sems.at[0]),
        pltpu.make_async_copy(own, planes.at[pl.ds(1, 2)], sems.at[1]),
        pltpu.make_async_copy(part.at[core], planes.at[3 - 3 * core], sems.at[2]),
        pltpu.make_async_copy(outer, planes.at[3 * core], sems.at[3]),
    ]
    for copy in copies:
        copy.start()
    info = row_info[...]
    for j in range(3):
        hot = pick_rows(info, j - 1)
        for half in range(2):
            pick[half, j * 128 : (j + 1) * 128, :] = hot[half * 128 : (half + 1) * 128, :]
    size = info.shape[1]
    clip_of = lax.broadcasted_iota(jnp.int32, (size, 128), 0) // 8
    lane = lax.broadcasted_iota(jnp.int32, (size, 128), 1)
    frames_of = jnp.broadcast_to(row_info[3:4, 0:128], (size, 128))
    rows_of = jnp.broadcast_to(row_info[4:5, 0:128], (size, 128))
    for h in range(2):
        for t in range(frame_count):
            inside = (clip_of == lane) & (frames_of > t) & (rows_of > meta[ROW_AT] + h)
            source = jnp.where(inside, 1.0, 0.0).astype(BF16)

            def store(t, half, row, source=source):
                belong[pl.ds(row, 128), :] = dot(pick[half, 128:256, :], source).astype(BF16)

            for half in range(2):

                @pl.when(half * 128 < meta[PAD + t])
                def _(t=t, half=half, store=store, h=h):
                    store(t, half, at16(h * s + meta[OFF + t] + half * 128))

        belong[pl.ds(at16(h * s + meta[END_AT]), 128), :] = jnp.zeros((128, 128), BF16)
    for copy in copies[1:]:
        copy.wait()
    for plane in range(4):

        def store(t, half, row, plane=plane):
            got = dot(pick[half], planes[plane, t]).astype(BF16)
            for j in range(3):
                packed[pl.ds(row, 128), j * 512 : (j + 1) * 512] = got[j * 128 : (j + 1) * 128, :]

        each_list(meta, plane * s, frame_count, store)
        packed[pl.ds(at16(plane * s + meta[END_AT]), 128), :] = jnp.zeros((128, 1536), BF16)
    copies[0].wait()
    blocks = meta[BLOCKS_AT]

    def conv(m, total):
        row = at128(m * 256)
        acc = dot(packed[pl.ds(row, 256), :], kernel[0:1536, :])
        acc += dot(packed[pl.ds(at128(s + row), 256), :], kernel[1536:3072, :])
        acc += dot(packed[pl.ds(at128(2 * s + row), 256), :], kernel[3072:4608, :])
        mid_pre[pl.ds(row, 256), :] = acc
        mask = jnp.sum(belong[pl.ds(row, 256), :].astype(F32), axis=1, keepdims=True)
        count, sums = total
        return count + jnp.sum(mask, axis=0, keepdims=True), sums + jnp.sum(acc * mask, axis=0, keepdims=True)

    count, sums = lax.fori_loop(0, blocks, conv, (jnp.zeros((1, 1), F32), jnp.zeros((1, 1152), F32)))
    center = sums / count

    def spread(m, total):
        row = at128(m * 256)
        mask = jnp.sum(belong[pl.ds(row, 256), :].astype(F32), axis=1, keepdims=True)
        off = (mid_pre[pl.ds(row, 256), :] - center) * mask
        return total + jnp.sum(off * off, axis=0, keepdims=True)

    squares = lax.fori_loop(0, blocks, spread, jnp.zeros((1, 1152), F32))
    stats[0:1, :] = jnp.broadcast_to(count, (1, 1152))
    stats[1:2, :] = sums
    stats[2:3, :] = squares
    stats[3:8, :] = jnp.zeros((5, 1152), F32)


def side_kernel(
    meta, row_info, own, own_low, part, outer, outer_part, turned, residual, planes, packed, pick, sems
):
    frame_count = own.shape[1]
    core = meta[CORE_AT]
    s = meta[S_AT]
    copies = [
        pltpu.make_async_copy(own, planes.at[pl.ds(1 + 2 * core, 2)], sems.at[0]),
        pltpu.make_async_copy(part, planes.at[pl.ds(3 - 2 * core, 2)], sems.at[1]),
        pltpu.make_async_copy(outer, planes.at[5 * core], sems.at[2]),
        pltpu.make_async_copy(outer_part, planes.at[5 - 5 * core], sems.at[3]),
    ]
    for copy in copies:
        copy.start()
    info = row_info[...]
    for j in range(3):
        hot = pick_rows(info, j - 1)
        for half in range(2):
            pick[half, j * 128 : (j + 1) * 128, :] = hot[half * 128 : (half + 1) * 128, :]
    for copy in copies:
        copy.wait()

    def plane_step(plane, carry):
        def store(t, half, row):
            got = dot(pick[half], planes[plane, t]).astype(BF16)
            for j in range(3):
                packed[pl.ds(row, 128), j * 512 : (j + 1) * 512] = got[j * 128 : (j + 1) * 128, :]

        each_list(meta, 0, frame_count, store)
        packed[pl.ds(at16(meta[END_AT]), 128), :] = jnp.zeros((128, 1536), BF16)

        def turn(m, carry):
            row = at128(m * 128)
            block = packed[pl.ds(row, 128), :].astype(F32)
            turned[:, pl.ds(at128(plane * s + row), 128)] = block.T.astype(BF16)
            return carry

        return lax.fori_loop(0, s // 128, turn, carry)

    lax.fori_loop(0, 6, plane_step, 0)
    for h in range(2):

        def store(t, half, row, h=h):
            hot = pick[half, 128:256, :]
            plane = 1 + 2 * core + h
            residual[pl.ds(row, 128), :] = dot(hot, planes[plane, t]) + dot(hot, own_low[h, t])

        each_list(meta, h * s, frame_count, store)
        residual[pl.ds(at16(h * s + meta[END_AT]), 128), :] = jnp.zeros((128, 512), F32)


def shift_lists(meta, frame_count, source, target, width, move):
    s = meta[S_AT]
    for h in range(2):

        def store(t, half, row, h=h):
            other = t + move
            if 0 <= other < frame_count:
                block = source(at16(h * s + meta[OFF + other] + half * 128))
                place = half * 128 + lax.broadcasted_iota(jnp.int32, (128, 1), 0)
                keep = jnp.where(place < meta[LEN + other], 1.0, 0.0).astype(BF16)
                target(row, block * keep)
            else:
                target(row, jnp.zeros((128, width), BF16))

        each_list(meta, h * s, frame_count, store)
        target(at16(h * s + meta[END_AT]), jnp.zeros((128, width), BF16))


def time_kernel(frame_count, meta, mid_pre, belong, coef, weight, mid_low, out_pre, stats, wide):
    blocks = meta[BLOCKS_AT]

    def act(m, carry):
        row = at128(m * 256)
        mask = jnp.sum(belong[pl.ds(row, 256), :].astype(F32), axis=1, keepdims=True)
        normed = (mid_pre[pl.ds(row, 256), :] - coef[0:1, :]) * coef[1:2, :]
        value = coef[2:3, :] * normed + coef[3:4, :]
        low = (value * sigmoid(value) * mask).astype(BF16)
        wide[pl.ds(row, 256), 1152:2304] = low
        mid_low[pl.ds(row, 256), :] = low
        return carry

    lax.fori_loop(0, blocks, act, 0)
    wide[pl.ds(at128(2 * meta[S_AT]), 256), :] = jnp.zeros((256, 3456), BF16)
    for k in (0, 2):

        def source(row):
            return wide[pl.ds(row, 128), 1152:2304]

        def target(row, value, k=k):
            wide[pl.ds(row, 128), k * 1152 : (k + 1) * 1152] = value

        shift_lists(meta, frame_count, source, target, 1152, k - 1)

    def conv(m, total):
        row = at128(m * 256)
        acc = dot(wide[pl.ds(row, 256), :], weight[...])
        out_pre[pl.ds(row, 256), :] = acc
        mask = jnp.sum(belong[pl.ds(row, 256), :].astype(F32), axis=1, keepdims=True)
        count, sums = total
        return count + jnp.sum(mask, axis=0, keepdims=True), sums + jnp.sum(acc * mask, axis=0, keepdims=True)

    count, sums = lax.fori_loop(0, blocks, conv, (jnp.zeros((1, 1), F32), jnp.zeros((1, 512), F32)))
    center = sums / count

    def spread(m, total):
        row = at128(m * 256)
        mask = jnp.sum(belong[pl.ds(row, 256), :].astype(F32), axis=1, keepdims=True)
        off = (out_pre[pl.ds(row, 256), :] - center) * mask
        return total + jnp.sum(off * off, axis=0, keepdims=True)

    squares = lax.fori_loop(0, blocks, spread, jnp.zeros((1, 512), F32))
    stats[0:1, :] = jnp.broadcast_to(count, (1, 512))
    stats[1:2, :] = sums
    stats[2:3, :] = squares
    stats[3:8, :] = jnp.zeros((5, 512), F32)


def act_kernel(meta, out_pre, belong, residual, coef, pooled_grad, act_grad, stats, pooled):
    blocks = meta[BLOCKS_AT]
    high, rest = split(pooled_grad[...])
    pooled[...] = jnp.zeros(pooled.shape, F32)

    def step(m, total):
        row = at128(m * 256)
        hot = belong[pl.ds(row, 256), :]
        normed = (out_pre[pl.ds(row, 256), :] - coef[0:1, :]) * coef[1:2, :]
        value = coef[2:3, :] * normed + coef[3:4, :] + residual[pl.ds(row, 256), :]
        s = sigmoid(value)
        first, second = split(value * s)
        pooled[...] += tn_dot(hot, first) + tn_dot(hot, second)
        grad = (dot(hot, high) + dot(hot, rest)) * (s * (1.0 + value * (1.0 - s)))
        act_grad[pl.ds(row, 256), :] = grad
        shift, gain = total
        return (
            shift + jnp.sum(grad, axis=0, keepdims=True),
            gain + jnp.sum(grad * normed, axis=0, keepdims=True),
        )

    zero = jnp.zeros((1, 512), F32)
    shift, gain = lax.fori_loop(0, blocks, step, (zero, zero))
    stats[0:1, :] = shift
    stats[1:2, :] = gain
    stats[2:8, :] = jnp.zeros((6, 512), F32)


def back_kernel(
    frame_count, meta, act_grad, out_pre, belong, out_coef, weight, mid_pre, mid_coef, wide, mid_act_grad, stats
):
    blocks = meta[BLOCKS_AT]

    def grad(m, carry):
        row = at128(m * 256)
        mask = jnp.sum(belong[pl.ds(row, 256), :].astype(F32), axis=1, keepdims=True)
        normed = (out_pre[pl.ds(row, 256), :] - out_coef[0:1, :]) * out_coef[1:2, :]
        inner = act_grad[pl.ds(row, 256), :] - mask * (out_coef[4:5, :] + normed * out_coef[5:6, :])
        wide[pl.ds(row, 256), 512:1024] = (out_coef[2:3, :] * out_coef[1:2, :] * inner).astype(BF16)
        return carry

    lax.fori_loop(0, blocks, grad, 0)
    wide[pl.ds(at128(2 * meta[S_AT]), 256), :] = jnp.zeros((256, 1536), BF16)
    for k in (0, 2):

        def source(row):
            return wide[pl.ds(row, 128), 512:1024]

        def target(row, value, k=k):
            wide[pl.ds(row, 128), k * 512 : (k + 1) * 512] = value

        shift_lists(meta, frame_count, source, target, 512, 1 - k)

    def conv(m, total):
        row = at128(m * 256)
        block = wide[pl.ds(row, 256), :]
        acc = nt_dot(block[:, 0:512], weight[0])
        acc += nt_dot(block[:, 512:1024], weight[1])
        acc += nt_dot(block[:, 1024:1536], weight[2])
        mask = jnp.sum(belong[pl.ds(row, 256), :].astype(F32), axis=1, keepdims=True)
        normed = (mid_pre[pl.ds(row, 256), :] - mid_coef[0:1, :]) * mid_coef[1:2, :]
        acc = acc * mask * slope(mid_coef[2:3, :] * normed + mid_coef[3:4, :])
        mid_act_grad[pl.ds(row, 256), :] = acc
        shift, gain = total
        return (
            shift + jnp.sum(acc, axis=0, keepdims=True),
            gain + jnp.sum(acc * normed, axis=0, keepdims=True),
        )

    zero = jnp.zeros((1, 1152), F32)
    shift, gain = lax.fori_loop(0, blocks, conv, (zero, zero))
    stats[0:1, :] = shift
    stats[1:2, :] = gain
    stats[2:8, :] = jnp.zeros((6, 1152), F32)


def time_grad_kernel(meta, mid_low, wide, out, total):
    blocks = meta[BLOCKS_AT]
    for k in range(3):
        total[...] = jnp.zeros(total.shape, F32)

        def step(m, carry, k=k):
            row = at128(m * 256)
            total[...] += tn_dot(mid_low[pl.ds(row, 256), :], wide[pl.ds(row, 256), k * 512 : (k + 1) * 512])
            return carry

        lax.fori_loop(0, blocks, step, 0)
        for lane in range(4):
            out[k, lane] = total[:, lane * 128 : (lane + 1) * 128].astype(BF16)


def mid_grad_kernel(meta, mid_act_grad, mid_pre, belong, coef, whole, keep, send):
    core = meta[CORE_AT]

    def step(m, carry):
        row = at128(m * 256)
        mask = jnp.sum(belong[pl.ds(row, 256), :].astype(F32), axis=1, keepdims=True)
        normed = (mid_pre[pl.ds(row, 256), :] - coef[0:1, :]) * coef[1:2, :]
        inner = mid_act_grad[pl.ds(row, 256), :] - mask * (coef[4:5, :] + normed * coef[5:6, :])
        low = (coef[2:3, :] * coef[1:2, :] * inner).astype(BF16)
        whole[pl.ds(row, 256), :] = low

        @pl.when(core == 0)
        def _():
            keep[pl.ds(row, 256), 0:512] = low[:, 0:512]
            send[pl.ds(row, 256), 0:512] = low[:, 512:1024]

        @pl.when(core != 0)
        def _():
            keep[pl.ds(row, 256), 0:512] = low[:, 512:1024]
            send[pl.ds(row, 256), 0:512] = low[:, 0:512]

        keep[pl.ds(row, 256), 512:640] = low[:, 1024:1152]
        send[pl.ds(row, 256), 512:640] = low[:, 1024:1152]
        return carry

    lax.fori_loop(0, meta[BLOCKS_AT], step, 0)


def space_grad_kernel(meta, turned, own, part, out, total):
    core = meta[CORE_AT]
    s = meta[S_AT]
    i = pl.program_id(1)
    total[...] = jnp.zeros(total.shape, F32)

    def step(m, carry):
        row = at128(m * 256)
        first = turned[:, pl.ds(at128((2 * core + i) * s + row), 256)]
        second = turned[:, pl.ds(at128((2 - 2 * core + i) * s + row), 256)]
        total[...] += dot(first, own[pl.ds(row, 256), :]) + dot(second, part[pl.ds(row, 256), :])
        return carry

    lax.fori_loop(0, meta[BLOCKS_AT], step, 0)
    for lane in range(4):
        out[0, lane * 512 : (lane + 1) * 512, :] = total[:, lane * 128 : (lane + 1) * 128].astype(BF16)

    @pl.when(core == 0)
    def _():
        out[0, 2048:2304, :] = total[0:256, 512:640].astype(BF16)

    @pl.when(core != 0)
    def _():
        out[0, 2048:2304, :] = total[256:512, 512:640].astype(BF16)


def input_back_kernel(
    frame_count, meta, col_info, grad, weight, act_grad, dense, edges, wide, spread, high, rest
):
    s = meta[S_AT]
    info = col_info[...]
    for j in range(3):
        spread[:, j * 256 : (j + 1) * 256] = pick_cols(info, j - 1)
    terms = {0: [(0, 0)], 1: [(0, 1), (1, 0)], 2: [(0, 2), (1, 1)], 3: [(1, 2)]}
    for plane in range(4):
        wide[plane, pl.ds(at128(s), 256), :] = jnp.zeros((256, 1536), BF16)

    def conv(m, carry):
        row = at128(m * 128)
        for plane in range(4):
            acc = None
            for h, i in terms[plane]:
                term = nt_dot(grad[pl.ds(at128(h * s + row), 128), :], weight[i * 1536 : (i + 1) * 1536, :])
                acc = term if acc is None else acc + term
            wide[plane, pl.ds(row, 128), :] = acc.astype(BF16)
        return carry

    lax.fori_loop(0, s // 128, conv, 0)

    def cut(m, carry):
        row = at128(m * 256)
        first, second = split(act_grad[pl.ds(row, 256), :])
        high[pl.ds(row, 256), :] = first
        rest[pl.ds(row, 256), :] = second
        return carry

    lax.fori_loop(0, meta[BLOCKS_AT], cut, 0)
    for part in (high, rest):
        part[pl.ds(at128(2 * s), 256), :] = jnp.zeros((256, 512), BF16)
    for plane in range(4):
        for t in range(frame_count):
            row = at16(meta[OFF + t])
            acc = None
            for j in range(3):
                term = dot(spread[:, j * 256 : (j + 1) * 256], wide[plane, pl.ds(row, 256), j * 512 : (j + 1) * 512])
                acc = term if acc is None else acc + term
            if plane == 0:
                edges[0, t] = acc.astype(BF16)
            elif plane == 3:
                edges[1, t] = acc.astype(BF16)
            else:
                row = at16((plane - 1) * s + meta[OFF + t])
                acc += dot(spread[:, 256:512], high[pl.ds(row, 256), :])
                acc += dot(spread[:, 256:512], rest[pl.ds(row, 256), :])
                dense[plane - 1, t] = acc


def join_kernel(meta, own, part, out):
    core = meta[CORE_AT]

    def place(first, second):
        for lane in range(4):
            out[0, :, lane * 128 : (lane + 1) * 128] = first[0, lane * 512 : (lane + 1) * 512, :].astype(F32)
            out[0, :, 512 + lane * 128 : 640 + lane * 128] = second[0, lane * 512 : (lane + 1) * 512, :].astype(F32)
        out[0, 0:256, 1024:1152] = first[0, 2048:2304, :].astype(F32)
        out[0, 256:512, 1024:1152] = second[0, 2048:2304, :].astype(F32)

    @pl.when(core == 0)
    def _():
        place(own, part)

    @pl.when(core != 0)
    def _():
        place(part, own)


def swap(value, axis, bit):
    size = lax.axis_size(axis)
    if size <= bit:
        return None
    return lax.ppermute(value, axis, [(i, i ^ bit) for i in range(size)])


def bits(axis):
    return [(axis, 1 << n) for n in range((lax.axis_size(axis) - 1).bit_length())]


def sum_all(value):
    for axis, bit in bits("sp") + bits("dp"):
        value = value + swap(value, axis, bit)
    return value


def merge_all(stats):
    for axis, bit in bits("sp") + bits("dp"):
        other = swap(stats, axis, bit)
        count = stats[0] + other[0]
        gap = stats[1] / stats[0] - other[1] / other[0]
        squares = stats[2] + other[2] + gap * gap * (stats[0] * other[0] / count)
        stats = jnp.stack([count, stats[1] + other[1], squares])
    return stats


def bit_of(axis, bit):
    return (lax.axis_index(axis) // bit) % 2


def halve(part, order):
    for axis, bit in order:
        n, rows, lanes = part.shape
        part = part.reshape(n, 2, rows // 2, lanes)
        mine = bit_of(axis, bit)
        send = lax.dynamic_index_in_dim(part, 1 - mine, 1, keepdims=False).astype(BF16)
        keep = lax.dynamic_index_in_dim(part, mine, 1, keepdims=False).astype(F32)
        part = keep + swap(send, axis, bit).astype(F32)
    return part.astype(BF16)


def double(part, order):
    for axis, bit in reversed(order):
        other = swap(part, axis, bit)
        mine = bit_of(axis, bit)
        low = jnp.where(mine == 0, part, other)
        high = jnp.where(mine == 0, other, part)
        part = jnp.concatenate([low, high], axis=1)
    return part


def shards(
    clip_input,
    space_weight,
    time_weight,
    gain_mid,
    shift_mid,
    gain_out,
    shift_out,
    class_weight,
    class_bias,
    frames,
    rows,
    cols,
    logit_grad,
):
    clip_count, frame_count, row_count, col_count, width = clip_input.shape
    middle = space_weight.shape[-1]
    classes = class_weight.shape[1]
    cells = clip_count * 8
    most = row_count * frame_count * clip_count * col_count
    sp_count = lax.axis_size("sp")
    core = lax.axis_index("sp") % 2
    row_start = lax.axis_index("sp") * row_count

    before = (frames[None, :] > frames[:, None]) | (
        (frames[None, :] == frames[:, None]) & (jnp.arange(clip_count)[None, :] < jnp.arange(clip_count)[:, None])
    )
    start = jnp.sum(jnp.where(before, cols[None, :], 0), axis=1)
    length = jnp.sum(jnp.where(frames[None, :] > jnp.arange(frame_count)[:, None], cols[None, :], 0), axis=1)
    padded = (length + 15) // 16 * 16
    offset = jnp.cumsum(padded) - padded
    end = jnp.sum(padded)
    plane = (end + 127) // 128 * 128
    meta = jnp.concatenate(
        [jnp.stack([plane, plane // 128, core, row_start]), offset, length, padded, end[None]]
    ).astype(jnp.int32)
    column = jnp.arange(8)[None, :]
    info = jnp.stack(
        [
            start[:, None] + column,
            jnp.broadcast_to(column, (clip_count, 8)),
            jnp.broadcast_to(cols[:, None], (clip_count, 8)),
            jnp.zeros((clip_count, 8), jnp.int32),
        ]
    ).reshape(4, cells)
    by_clip = jnp.zeros((2, cells), jnp.int32).at[:, :clip_count].set(jnp.stack([frames, rows]))
    row_info = jnp.concatenate([info[:3], by_clip, jnp.zeros((3, cells), jnp.int32)]).astype(jnp.int32)
    col_info = jnp.concatenate([info, info], axis=0).T.astype(jnp.int32)

    frame_ok = jnp.arange(frame_count)[None, :] < frames[:, None]
    row_ok = (row_start + jnp.arange(row_count))[None, :] < rows[:, None]
    col_ok = jnp.arange(col_count)[None, :] < cols[:, None]
    mask = (frame_ok[:, :, None, None] & row_ok[:, None, :, None] & col_ok[:, None, None, :])[..., None]
    masked = jnp.where(mask, clip_input, 0.0)
    masked = jnp.pad(masked.transpose(2, 1, 0, 3, 4), ((0, 0), (0, 0), (0, 0), (0, 8 - col_count), (0, 0)))
    masked = masked.reshape(row_count, frame_count, cells, width)
    rounded = lax.reduce_precision(masked, 8, 7)
    own = rounded.astype(BF16)
    own_low = (masked - rounded).astype(BF16)
    part = swap(own, "sp", 1)
    ahead = [(i, i + 1 if i % 2 else i - 1) for i in range(sp_count)]
    outer = lax.ppermute(
        lax.dynamic_index_in_dim(own, core, 0, keepdims=False),
        "sp",
        [(i, j) for i, j in ahead if 0 <= j < sp_count],
    )
    outer_part = swap(outer, "sp", 1)

    weight = space_weight.reshape(9 * width, middle)
    mid_pre, belong, stats = pl.pallas_call(
        space_kernel,
        out_shape=(
            jax.ShapeDtypeStruct((most, middle), F32),
            jax.ShapeDtypeStruct((most + 256, 128), BF16),
            jax.ShapeDtypeStruct((8, middle), F32),
        ),
        in_specs=[SM, VM, ANY, ANY, ANY, ANY],
        out_specs=(VM, VM, VM),
        scratch_shapes=[
            pltpu.VMEM((4, frame_count, cells, width), BF16),
            pltpu.VMEM((2 * most + 256, 3 * width), BF16),
            pltpu.VMEM((9 * width, middle), BF16),
            pltpu.VMEM((2, 384, cells), BF16),
            pltpu.SemaphoreType.DMA((4,)),
        ],
        compiler_params=params(40),
        name="space_conv",
    )(meta, row_info, own, part, outer, weight)

    turned, residual = pl.pallas_call(
        side_kernel,
        out_shape=(
            jax.ShapeDtypeStruct((3 * width, 3 * most), BF16),
            jax.ShapeDtypeStruct((most + 256, width), F32),
        ),
        in_specs=[SM, VM, ANY, VM, ANY, ANY, ANY],
        out_specs=(VM, VM),
        scratch_shapes=[
            pltpu.VMEM((6, frame_count, cells, width), BF16),
            pltpu.VMEM((most // 2 + 256, 3 * width), BF16),
            pltpu.VMEM((2, 384, cells), BF16),
            pltpu.SemaphoreType.DMA((4,)),
        ],
        compiler_params=params(38),
        name="side",
    )(meta, row_info, own, own_low, part, outer, outer_part)

    clip_cells = (frames * rows * cols).astype(F32)
    pooled_grad = jnp.dot(logit_grad, class_weight.T, precision=HIGH) / clip_cells[:, None]
    pooled_grad = jnp.pad(pooled_grad, ((0, 128 - clip_count), (0, 0)))

    merged = merge_all(stats[:3])
    count_all = merged[0, 0]
    mid_coef = jnp.stack(
        [merged[1] / merged[0], lax.rsqrt(merged[2] / merged[0] + EPSILON), gain_mid, shift_mid]
    )
    mid_low, out_pre, stats = pl.pallas_call(
        functools.partial(time_kernel, frame_count),
        out_shape=(
            jax.ShapeDtypeStruct((most, middle), BF16),
            jax.ShapeDtypeStruct((most, width), F32),
            jax.ShapeDtypeStruct((8, width), F32),
        ),
        in_specs=[SM, VM, VM, VM, VM],
        out_specs=(VM, VM, VM),
        scratch_shapes=[pltpu.VMEM((most + 256, 3 * middle), BF16)],
        compiler_params=params(38),
        name="time_conv",
    )(meta, mid_pre, belong, mid_coef, time_weight.reshape(3 * middle, width))

    merged = merge_all(stats[:3])
    out_coef = jnp.stack(
        [merged[1] / merged[0], lax.rsqrt(merged[2] / merged[0] + EPSILON), gain_out, shift_out]
    )
    act_grad, stats, pooled_sum = pl.pallas_call(
        act_kernel,
        out_shape=(
            jax.ShapeDtypeStruct((most, width), F32),
            jax.ShapeDtypeStruct((8, width), F32),
            jax.ShapeDtypeStruct((128, width), F32),
        ),
        in_specs=[SM, VM, VM, VM, VM, VM],
        out_specs=(VM, VM, VM),
        compiler_params=params(16),
        name="act",
    )(meta, out_pre, belong, residual, out_coef, pooled_grad)

    first = (lax.axis_index("sp") == 0).astype(F32)
    bias_part = jnp.pad(jnp.sum(logit_grad, axis=0) * first, (0, width - classes))
    sums = sum_all(jnp.concatenate([stats[:2], bias_part[None]]))
    shift_out_grad, gain_out_grad, class_bias_grad = sums[0], sums[1], sums[2, :classes]
    pooled_own = pooled_sum[:clip_count] / clip_cells[:, None]
    logits = jnp.dot(pooled_own, class_weight, precision=HIGH)
    for axis, bit in bits("sp"):
        logits = logits + swap(logits, axis, bit)
    logits = logits + class_bias
    class_part = jnp.dot(pooled_own.T, logit_grad, precision=HIGH)

    out_coef = jnp.concatenate([out_coef, sums[:2] / count_all])
    wide, mid_act_grad, stats = pl.pallas_call(
        functools.partial(back_kernel, frame_count),
        out_shape=(
            jax.ShapeDtypeStruct((most + 256, 3 * width), BF16),
            jax.ShapeDtypeStruct((most, middle), F32),
            jax.ShapeDtypeStruct((8, middle), F32),
        ),
        in_specs=[SM, VM, VM, VM, VM, VM, VM, VM],
        out_specs=(VM, VM, VM),
        compiler_params=params(39),
        name="time_back",
    )(meta, act_grad, out_pre, belong, out_coef, time_weight, mid_pre, mid_coef)

    time_part = pl.pallas_call(
        time_grad_kernel,
        out_shape=jax.ShapeDtypeStruct((3, 4, middle, 128), BF16),
        in_specs=[SM, VM, VM],
        out_specs=VM,
        scratch_shapes=[pltpu.VMEM((middle, width), F32)],
        compiler_params=params(21),
        name="time_grad",
    )(meta, mid_low, wide)

    sums = sum_all(stats[:2])
    shift_mid_grad, gain_mid_grad = sums[0], sums[1]
    mid_coef = jnp.concatenate([mid_coef, sums / count_all])
    mid_grad, keep, send = pl.pallas_call(
        mid_grad_kernel,
        out_shape=(
            jax.ShapeDtypeStruct((most, middle), BF16),
            jax.ShapeDtypeStruct((most, 640), BF16),
            jax.ShapeDtypeStruct((most, 640), BF16),
        ),
        in_specs=[SM, VM, VM, VM, VM],
        out_specs=(VM, VM, VM),
        compiler_params=params(30),
        name="mid_grad",
    )(meta, mid_act_grad, mid_pre, belong, mid_coef)
    other = swap(send, "sp", 1)

    space_part = pl.pallas_call(
        space_grad_kernel,
        grid_spec=pltpu.PrefetchScalarGridSpec(
            num_scalar_prefetch=1,
            grid=(3, 3),
            in_specs=[
                pl.BlockSpec((width, 3 * most), lambda j, i, meta: (j, 0)),
                pl.BlockSpec((most, 640), lambda j, i, meta: (0, 0)),
                pl.BlockSpec((most, 640), lambda j, i, meta: (0, 0)),
            ],
            out_specs=pl.BlockSpec((1, 2304, 128), lambda j, i, meta: (3 * j + i, 0, 0)),
            scratch_shapes=[pltpu.VMEM((width, 640), F32)],
        ),
        out_shape=jax.ShapeDtypeStruct((9, 2304, 128), BF16),
        compiler_params=params(28),
        name="space_grad",
    )(meta, turned, keep, other)

    dense, edges = pl.pallas_call(
        functools.partial(input_back_kernel, frame_count),
        out_shape=(
            jax.ShapeDtypeStruct((row_count, frame_count, cells, width), F32),
            jax.ShapeDtypeStruct((2, frame_count, cells, width), BF16),
        ),
        in_specs=[SM, VM, VM, VM, VM],
        out_specs=(VM, VM),
        scratch_shapes=[
            pltpu.VMEM((4, most // 2 + 256, 3 * width), BF16),
            pltpu.VMEM((cells, 3 * cells), BF16),
            pltpu.VMEM((most + 256, width), BF16),
            pltpu.VMEM((most + 256, width), BF16),
        ],
        compiler_params=params(48),
        name="input_back",
    )(meta, col_info, mid_grad, weight, act_grad)
    up = lax.ppermute(edges[0], "sp", [(i, i - 1) for i in range(1, sp_count)])
    down = lax.ppermute(edges[1], "sp", [(i, i + 1) for i in range(sp_count - 1)])
    input_grad = dense + jnp.stack([down, up]).astype(F32)
    input_grad = input_grad.reshape(row_count, frame_count, clip_count, 8, width)[:, :, :, :col_count]
    input_grad = jnp.where(mask, input_grad.transpose(2, 1, 0, 3, 4), 0.0)

    x_bits, y_bits, z_bits = bits("sp")[1:], bits("dp")[:1], bits("dp")[1:]
    order_a = x_bits + y_bits + z_bits
    order_b = y_bits + x_bits + z_bits
    order_c = z_bits + x_bits + y_bits
    parts = []
    for low, high, order in ((0, 4, order_a), (4, 8, order_b), (8, 9, order_c)):
        parts.append(double(halve(space_part[low:high], order), order))
    gathered = jnp.concatenate(parts)
    gathered_part = swap(gathered, "sp", 1)
    space_grad = pl.pallas_call(
        join_kernel,
        grid_spec=pltpu.PrefetchScalarGridSpec(
            num_scalar_prefetch=1,
            grid=(9,),
            in_specs=[
                pl.BlockSpec((1, 2304, 128), lambda n, meta: (n % 3 * 3 + n // 3, 0, 0)),
                pl.BlockSpec((1, 2304, 128), lambda n, meta: (n % 3 * 3 + n // 3, 0, 0)),
            ],
            out_specs=pl.BlockSpec((1, width, middle), lambda n, meta: (n, 0, 0)),
        ),
        out_shape=jax.ShapeDtypeStruct((9, width, middle), F32),
        compiler_params=params(24),
        name="join",
    )(meta, gathered, gathered_part).reshape(3, 3, width, middle)

    class_rows = jnp.pad(class_part, ((0, 0), (0, 512 - classes))).astype(BF16)
    class_rows = class_rows.reshape(width, 4, 128).transpose(1, 0, 2).reshape(1, 4 * width, 128)
    small = jnp.concatenate([time_part.reshape(1, 12 * middle, 128), class_rows], axis=1)
    order = bits("sp")[:1] + order_b
    small = double(halve(small, order), order)
    time_grad = small[0, : 12 * middle].reshape(3, 4, middle, 128).transpose(0, 2, 1, 3)
    time_grad = time_grad.reshape(3, middle, width).astype(F32)
    class_weight_grad = small[0, 12 * middle :].reshape(4, width, 128).transpose(1, 0, 2)
    class_weight_grad = class_weight_grad.reshape(width, 512)[:, :classes].astype(F32)
    return (
        logits,
        input_grad,
        space_grad,
        time_grad,
        gain_mid_grad,
        shift_mid_grad,
        gain_out_grad,
        shift_out_grad,
        class_weight_grad,
        class_bias_grad,
    )


def solution(mesh):
    placed = (
        P("dp", None, "sp", None, None),
        P(),
        P(),
        P(),
        P(),
        P(),
        P(),
        P(),
        P(),
        P("dp"),
        P("dp"),
        P("dp"),
        P("dp", None),
    )
    return jax.shard_map(
        shards,
        mesh=mesh,
        in_specs=placed,
        out_specs=(
            P("dp", None),
            P("dp", None, "sp", None, None),
            P(),
            P(),
            P(),
            P(),
            P(),
            P(),
            P(),
            P(),
        ),
        check_vma=False,
    )
```

time: 1030 us -> 568 us (0.55)
  blocking collectives: 265 us -> 0 us
  matrix products: 220 us -> 3.56 us
  waiting for transfers between devices: 333 us -> 182 us
  Pallas kernels: 0 us -> 143 us
  starting transfers between devices: 9.17 us -> 95.4 us
  local copies, waits for them, and re-layouts: 101 us -> 64.1 us
  between operations: 16.4 us -> 3.05 us
  other arithmetic: 80.4 us -> 67.6 us
    psum x7 -> x0, blocking collectives: 265 us -> none  [the longest x2 82 us: norm_stats(): lax.psum((local_count, jnp.sum(values * mask, axis=(0, 1, 2, 3))), ('dp',...]
    reduce_scatter x1 -> x0, waiting for transfers between devices: 264 us -> none  [shards(): lax.psum_scatter(pack_flat([space_grad, time_grad]), ('dp', 'sp'), scatte...]
    dot_general x38 -> x2, matrix products: 219 us -> 2.35 us  [the longest x1 1.48 us: shards(): logits = jnp.dot(pooled_own, class_weight, precision=HIGH)]
    ppermute x4 -> x63, waiting for transfers between devices: 0.01 us -> 182 us  [the longest x60 182 us: swap(): return lax.ppermute(value, axis, [(i, i ^ bit) for i in range(size)])]
    pallas_call x0 -> x10, Pallas kernels: none -> 143 us  [the longest x1 32.3 us: shards(): pl.pallas_call(functools.partial(input_back_kernel, frame_count), out_sha...]
    ppermute x4 -> x63, starting transfers between devices: 9 us -> 95.4 us  [the longest x60 89.6 us: swap(): return lax.ppermute(value, axis, [(i, i ^ bit) for i in range(size)])]
    all_gather x1 -> x0, waiting for transfers between devices: 68.6 us -> none  [shards(): lax.all_gather(both_share, ('dp', 'sp'), axis=0, tiled=True)]
    reshape x3 -> x0, local copies, waits for them, and re-layouts: 53.6 us -> none  [the longest x2 31.7 us: unpack_flat(): pieces.append(flat[offset:offset + length].reshape(dims))]
  transfers between devices with their start and end apart: 8 -> 63, of which waited for: 2 -> 43; matrix products, arithmetic and copies ran while one was open for 15% -> 16% of each run, Pallas kernels for 0% -> 15%
where the time goes in v1:
time: 568 us; the launch traced here: 559 us
  waiting for transfers between devices  182 us (32%)
  Pallas kernels  143 us (25%)
  starting transfers between devices  95.4 us (17%)
  other arithmetic  67.6 us (12%)
  local copies, waits for them, and re-layouts  64.1 us (11%)
    ppermute x60, waiting for transfers between devices, swap(): return lax.ppermute(value, axis, [(i, i ^ bit) for i in range(size)])  182 us
    ppermute x60, starting transfers between devices, swap(): return lax.ppermute(value, axis, [(i, i ^ bit) for i in range(size)])  89.6 us
    unnamed x116, local copies, waits for them, and re-layouts  43.7 us
    pallas_call x1, Pallas kernels, shards(): pl.pallas_call(functools.partial(input_back_kernel, frame_count), out_sha...  32.3 us
    pallas_call x1, Pallas kernels, shards(): pl.pallas_call(side_kernel, out_shape=(jax.ShapeDtypeStruct((3 * width, 3...  20.9 us
    pallas_call x1, Pallas kernels, shards(): pl.pallas_call(space_kernel, out_shape=(jax.ShapeDtypeStruct((most, middl...  20.1 us
    pallas_call x1, Pallas kernels, shards(): pl.pallas_call(space_grad_kernel, grid_spec=pltpu.PrefetchScalarGridSpec(...  17.6 us
    pallas_call x1, Pallas kernels, shards(): pl.pallas_call(functools.partial(back_kernel, frame_count), out_shape=(ja...  14.8 us
  transfers between devices with their start and end apart: 63, of which 43 were waited for; matrix products, arithmetic and copies ran while one was open for 16% of the time, Pallas kernels for 15%

profile of v1, /device:TPU:0, one launch (start us, length us, event | category | flops | bytes accessed | tf_op | source)
XLA Modules:
  0.0 559.0 jit_solution(3678699398382138270)
XLA Ops:
  18.7 20.1 %space_conv.1 = (f32[1792,1152]{1,0:T(8,128)S(1)}, bf16[2048,128]{1,0:T(8,128)(2,1)S(1)}, f32[8,1152]{1,0:T(8,128)S(1)}) custom-call(s32[17]{0:T(128)S(1)} %concatenate.84.meta, s32[8,256]{1,0:T(8,128)S(1)} %concatenate.85.row_info, bf16[2,4,256,512]{3,2,1,0:T(8,128)(2,1)S(1)} %get-tuple-element.127.own, bf16[2,4,256,512]{3,2,1,0:T(8,128)(2,1)} %collective-permute-done.part, ...), custom_call_target="tpu_custom_call" | custom-call | tf_op jit(solution)/shard_map/space_conv/pallas_call | solution.py:621
  42.1 11.1 %collective-permute-start.2 = (f32[3,1152]{1,0:T(4,128)S(1)}, f32[3,1152]{1,0:T(4,128)S(1)}, u32[]{:S(2)}, u32[]{:S(2)}) collective-permute-start(f32[3,1152]{1,0:T(4,128)S(1)} %slice.233), channel_id=1, source_target_pairs={{0,1},{1,0},{2,3},{3,2},{4,5},{5,4},{6,7},{7,6},{8,9},{9,8},{10,11... | collective-permute-start | bytes 41480 | tf_op jit(solution)/shard_map/ppermute | solution.py:504
  72.1 10.7 %time_conv.1 = (bf16[1792,1152]{1,0:T(8,128)(2,1)S(1)}, f32[1792,512]{1,0:T(8,128)S(1)}, f32[8,512]{1,0:T(8,128)S(1)}) custom-call(s32[17]{0:T(128)S(1)} %concatenate.84.meta, f32[1792,1152]{1,0:T(8,128)} %copy-done.2, bf16[2048,128]{1,0:T(8,128)(2,1)S(1)} %get-tuple-element.42.belong, f32[4,1152]{1,0:T(4,128)S(1)} %pad_maximum_fusion.19.coef.mid_coef, ...), custom_call_target="tpu_custom_call" | custom-call | tf_op jit(solution)/shard_map/time_conv/pallas_call | solution.py:668
  106.9 20.9 %side.1 = (bf16[1536,5376]{1,0:T(8,128)(2,1)}, f32[2048,512]{1,0:T(8,128)S(1)}) custom-call(s32[17]{0:T(128)S(1)} %concatenate.84.meta, s32[8,256]{1,0:T(8,128)S(1)} %concatenate.85.row_info, bf16[2,4,256,512]{3,2,1,0:T(8,128)(2,1)S(1)} %get-tuple-element.127.own, bf16[2,4,256,512]{3,2,1,0:T(8,128)(2,1)S(1)} %copy-done.12, ...), custom_call_target="tpu_custom_call" | custom-call | tf_op jit(solution)/shard_map/side/pallas_call | solution.py:641
  157.6 14.8 %time_back.1 = (bf16[2048,1536]{1,0:T(8,128)(2,1)}, f32[1792,1152]{1,0:T(8,128)}, f32[8,1152]{1,0:T(8,128)S(1)}) custom-call(s32[17]{0:T(128)S(1)} %concatenate.84.meta, f32[1792,512]{1,0:T(8,128)S(1)} %copy-done.8, f32[1792,512]{1,0:T(8,128)S(1)} %copy-done.6, bf16[2048,128]{1,0:T(8,128)(2,1)S(1)} %get-tuple-element.42.belong, ...), custom_call_target="tpu_custom_call" | custom-call | tf_op jit(solution)/shard_map/time_back/pallas_call | solution.py:711
  192.7 6.3 %time_grad.1 = bf16[3,4,1152,128]{3,2,1,0:T(8,128)(2,1)S(1)} custom-call(s32[17]{0:T(128)S(1)} %concatenate.84.meta, bf16[1792,1152]{1,0:T(8,128)(2,1)S(1)} %copy-done.18, bf16[2048,1536]{1,0:T(8,128)(2,1)S(1)} %copy-done.16), custom_call_target="tpu_custom_call" | custom-call | tf_op jit(solution)/shard_map/time_grad/pallas_call | solution.py:724
  212.8 9.1 %pad_maximum_fusion = bf16[1,15872,128]{2,1,0:T(8,128)(2,1)S(1)} fusion(bf16[1,2048,128]{2,1,0:T(8,128)(2,1)S(1)} %bitcast.213, bf16[1,13824,128]{2,1,0:T(8,128)(2,1)S(1)} %bitcast.182), kind=kLoop, calls=%fused_computation.7 | loop fusion | flops 8126464 | bytes 8126464 | tf_op jit(solution)/shard_map/concatenate | solution.py:819
  226.8 32.3 %input_back.1 = (f32[2,4,256,512]{3,2,1,0:T(8,128)}, bf16[2,4,256,512]{3,2,1,0:T(8,128)(2,1)S(1)}) custom-call(s32[17]{0:T(128)S(1)} %concatenate.84.meta, s32[256,8]{1,0:T(8,128)S(1)} %bitcast.184, bf16[1792,1152]{1,0:T(8,128)(2,1)} %copy-done.19, bf16[4608,1152]{1,0:T(8,128)(2,1)} %bitcast.186, f32[1792,512]{1,0:T(8,128)S(1)} %copy-done.9), custom_call_target="tpu_custom_call" | custom-call | tf_op jit(solution)/shard_map/input_back/pallas_call | solution.py:769
  270.5 17.6 %space_grad.1 = bf16[9,2304,128]{2,1,0:T(8,128)(2,1)S(1)} custom-call(s32[17]{0:T(128)S(1)} %concatenate.84.meta, bf16[1536,5376]{1,0:T(8,128)(2,1)S(1)} %copy-done.3, bf16[1792,640]{1,0:T(8,128)(2,1)S(1)} %get-tuple-element.56.own, bf16[1792,640]{1,0:T(8,128)(2,1)S(1)} %collective-permute-done.27.part), custom_call_target="tpu_custom_call" | custom-call | tf_op jit(solution)/shard_map/space_grad/pallas_call | solution.py:751
  291.5 6.2 %collective-permute-done.44 = bf16[1,1152,128]{2,1,0:T(8,128)(2,1)S(1)} collective-permute-done((bf16[1,1152,128]{2,1,0:T(8,128)(2,1)S(1)}, bf16[1,1152,128]{2,1,0:T(8,128)(2,1)S(1)}, u32[]{:S(2)}, u32[]{:S(2)}) %collective-permute-start.44) | collective-permute-done | bytes 294944 | tf_op jit(solution)/shard_map/ppermute | solution.py:504
  319.1 18.8 %collective-permute-done.48 = bf16[1,144,128]{2,1,0:T(8,128)(2,1)S(1)} collective-permute-done((bf16[1,144,128]{2,1,0:T(8,128)(2,1)S(1)}, bf16[1,144,128]{2,1,0:T(8,128)(2,1)S(1)}, u32[]{:S(2)}, u32[]{:S(2)}) %collective-permute-start.48) | collective-permute-done | bytes 36896 | tf_op jit(solution)/shard_map/ppermute | solution.py:504
  343.5 6.6 %collective-permute-done.50 = bf16[1,576,128]{2,1,0:T(8,128)(2,1)S(1)} collective-permute-done((bf16[1,576,128]{2,1,0:T(8,128)(2,1)S(1)}, bf16[1,576,128]{2,1,0:T(8,128)(2,1)S(1)}, u32[]{:S(2)}, u32[]{:S(2)}) %collective-permute-start.50) | collective-permute-done | bytes 147488 | tf_op jit(solution)/shard_map/ppermute | solution.py:504
  357.4 18.3 %collective-permute-done.55 = bf16[1,1984,128]{2,1,0:T(8,128)(2,1)S(1)} collective-permute-done((bf16[1,1984,128]{2,1,0:T(8,128)(2,1)S(1)}, bf16[1,1984,128]{2,1,0:T(8,128)(2,1)S(1)}, u32[]{:S(2)}, u32[]{:S(2)}) %collective-permute-start.55) | collective-permute-done | bytes 507936 | tf_op jit(solution)/shard_map/ppermute | solution.py:504
  387.0 6.3 %collective-permute-done.57 = bf16[1,496,128]{2,1,0:T(8,128)(2,1)S(1)} collective-permute-done((bf16[1,496,128]{2,1,0:T(8,128)(2,1)S(1)}, bf16[1,496,128]{2,1,0:T(8,128)(2,1)S(1)}, u32[]{:S(2)}, u32[]{:S(2)}) %collective-permute-start.57) | collective-permute-done | bytes 127008 | tf_op jit(solution)/shard_map/ppermute | solution.py:504
  404.5 6.6 %collective-permute-start.38 = (bf16[4,288,128]{2,1,0:T(8,128)(2,1)S(1)}, bf16[4,288,128]{2,1,0:T(8,128)(2,1)S(1)}, u32[]{:S(2)}, u32[]{:S(2)}) collective-permute-start(bf16[4,288,128]{2,1,0:T(8,128)(2,1)S(1)} %fusion.7), channel_id=1, source_target_pairs={{0,8},{4,12},{8,0},{12,4},{16,24},{20,28},{24,16},{28,20},{1,9},{5... | collective-permute-start | bytes 884744 | tf_op jit(solution)/shard_map/ppermute | solution.py:504
  422.3 6.0 %collective-permute-done.31 = bf16[4,144,128]{2,1,0:T(8,128)(2,1)S(1)} collective-permute-done((bf16[4,144,128]{2,1,0:T(8,128)(2,1)S(1)}, bf16[4,144,128]{2,1,0:T(8,128)(2,1)S(1)}, u32[]{:S(2)}, u32[]{:S(2)}) %collective-permute-start.31) | collective-permute-done | bytes 147488 | tf_op jit(solution)/shard_map/ppermute | solution.py:504
  448.6 11.1 %collective-permute-done.34 = bf16[4,576,128]{2,1,0:T(8,128)(2,1)S(1)} collective-permute-done((bf16[4,576,128]{2,1,0:T(8,128)(2,1)S(1)}, bf16[4,576,128]{2,1,0:T(8,128)(2,1)S(1)}, u32[]{:S(2)}, u32[]{:S(2)}) %collective-permute-start.34) | collective-permute-done | bytes 589856 | tf_op jit(solution)/shard_map/ppermute | solution.py:504
  463.5 17.9 %collective-permute-done.61 = bf16[1,3968,128]{2,1,0:T(8,128)(2,1)S(1)} collective-permute-done((bf16[1,3968,128]{2,1,0:T(8,128)(2,1)S(1)}, bf16[1,3968,128]{2,1,0:T(8,128)(2,1)S(1)}, u32[]{:S(2)}, u32[]{:S(2)}) %collective-permute-start.61) | collective-permute-done | bytes 1015840 | tf_op jit(solution)/shard_map/ppermute | solution.py:504
  482.6 15.4 %collective-permute-done.43 = bf16[4,1152,128]{2,1,0:T(8,128)(2,1)S(1)} collective-permute-done((bf16[4,1152,128]{2,1,0:T(8,128)(2,1)S(1)}, bf16[4,1152,128]{2,1,0:T(8,128)(2,1)S(1)}, u32[]{:S(2)}, u32[]{:S(2)}) %collective-permute-start.43) | collective-permute-done | bytes 1179680 | tf_op jit(solution)/shard_map/ppermute | solution.py:504
  498.4 10.8 %maximum_maximum_fusion.own = bf16[9,2304,128]{2,1,0:T(8,128)(2,1)} fusion(bf16[1,1152,128]{2,1,0:T(8,128)(2,1)S(1)} %get-tuple-element.149, bf16[1,1152,128]{2,1,0:T(8,128)(2,1)S(1)} %get-tuple-element.148, bf16[4,1152,128]{2,1,0:T(8,128)(2,1)S(1)} %get-tuple-element.133, bf16[4,1152,128]{2,1,0:T(8,128)(2,1)S(1)} %get-tuple-element.132, ...), kind=kLoop, calls=%fused_computation.3 | loop fusion | flops 31850496 | bytes 10616832 | tf_op jit(solution)/shard_map/concatenate | solution.py:799
  515.7 9.2 %pad_maximum_fusion.1 = bf16[1,13824,128]{2,1,0:T(8,128)(2,1)S(1)} fusion(bf16[1,7936,128]{2,1,0:T(8,128)(2,1)S(1)} %get-tuple-element.129, bf16[1,7936,128]{2,1,0:T(8,128)(2,1)} %get-tuple-element.128), kind=kLoop, calls=%fused_computation.12 | loop fusion | flops 7077888 | bytes 7602176 | tf_op jit(solution)/shard_map/concatenate | solution.py:548
  528.5 8.0 %copy.92 = f32[3,1152,4,128]{1,3,2,0:T(8,128)} copy(f32[3,1152,4,128]{3,1,2,0:T(8,128)} %convert_bitcast_fusion) | data formatting | bytes 14155776 | tf_op jit(solution)/shard_map/convert_element_type | solution.py:823
  536.5 8.0 %copy.94 = f32[3,1152,512]{2,1,0:T(8,128)} copy(f32[3,1152,512]{1,2,0:T(8,128)} %bitcast.187) | data formatting | bytes 14155776
  545.5 13.1 %join.1 = f32[9,512,1152]{2,1,0:T(8,128)} custom-call(s32[17]{0:T(128)S(1)} %concatenate.84.meta, bf16[9,2304,128]{2,1,0:T(8,128)(2,1)} %maximum_maximum_fusion.own, bf16[9,2304,128]{2,1,0:T(8,128)(2,1)} %collective-permute-done.52.part), custom_call_target="tpu_custom_call" | custom-call | tf_op jit(solution)/shard_map/join/pallas_call | solution.py:801
  (395 shorter events, 250.7 us)
Async XLA Ops:
  101.4 26.4 %collective-permute-start.12 = (f32[3,512]{1,0:T(4,128)S(1)}, f32[3,512]{1,0:T(4,128)S(1)}, u32[]{:S(2)}, u32[]{:S(2)}) collective-permute-start(f32[3,512]{1,0:T(4,128)S(1)} %pad_maximum_fusion.23), channel_id=1, source_target_pairs={{0,16},{4,20},{8,24},{12,28},{16,0},{20,4},{24,8},{28,12},{1,17},{... | collective-permute-start | bytes 18440 | tf_op jit(solution)/shard_map/ppermute | solution.py:504
  185.2 13.7 %collective-permute-start.24 = (f32[2,1152]{1,0:T(2,128)}, f32[2,1152]{1,0:T(2,128)}, u32[]{:S(2)}, u32[]{:S(2)}) collective-permute-start(f32[2,1152]{1,0:T(2,128)} %add.678), channel_id=1, source_target_pairs={{0,16},{4,20},{8,24},{12,28},{16,0},{20,4},{24,8},{28,12},{1,17},{... | collective-permute-start | bytes 27656 | tf_op jit(solution)/shard_map/ppermute | solution.py:504
  186.6 37.2 %collective-permute-start.13 = (f32[32,400]{1,0:T(8,128)}, f32[32,400]{1,0:T(8,128)}, u32[]{:S(2)}, u32[]{:S(2)}) collective-permute-start(f32[32,400]{1,0:T(8,128)} %fusion.21), channel_id=1, source_target_pairs={{0,1},{1,0},{2,3},{3,2},{4,5},{5,4},{6,7},{7,6},{8,9},{9,8},{10,11... | collective-permute-start | bytes 153608 | tf_op jit(solution)/shard_map/ppermute | solution.py:504
  212.2 52.5 %collective-permute-start.27 = (bf16[1792,640]{1,0:T(8,128)(2,1)S(1)}, bf16[1792,640]{1,0:T(8,128)(2,1)S(1)}, u32[]{:S(2)}, u32[]{:S(2)}) collective-permute-start(bf16[1792,640]{1,0:T(8,128)(2,1)S(1)} %get-tuple-element.57), channel_id=1, source_target_pairs={{0,1},{1,0},{2,3},{3,2},{4,5},{5,4},{6,7},{7,6},{8,9},{9,8},{10,11... | collective-permute-start | bytes 6881288 | tf_op jit(solution)/shard_map/ppermute | solution.py:504
  223.8 85.0 %collective-permute-start.53 = (bf16[1,7936,128]{2,1,0:T(8,128)(2,1)S(1)}, bf16[1,7936,128]{2,1,0:T(8,128)(2,1)}, u32[]{:S(2)}, u32[]{:S(2)}) collective-permute-start(bf16[1,7936,128]{2,1,0:T(8,128)(2,1)S(1)} %dynamic-slice_bitcast_fusion), channel_id=1, source_target_pairs={{0,1},{1,0},{2,3},{3,2},{4,5},{5,4},{6,7},{7,6},{8,9},{9,8},{10,11... | collective-permute-start | bytes 6094856 | tf_op jit(solution)/shard_map/ppermute | solution.py:504
  225.4 65.5 %collective-permute-start.14 = (f32[32,400]{1,0:T(8,128)S(1)}, f32[32,400]{1,0:T(8,128)S(1)}, u32[]{:S(2)}, u32[]{:S(2)}) collective-permute-start(f32[32,400]{1,0:T(8,128)S(1)} %add.666), channel_id=1, source_target_pairs={{0,2},{1,3},{2,0},{3,1},{4,6},{5,7},{6,4},{7,5},{8,10},{9,11},{10,... | collective-permute-start | bytes 153608 | tf_op jit(solution)/shard_map/ppermute | solution.py:504
  260.6 39.7 %collective-permute-start.25 = (bf16[4,256,512]{2,1,0:T(8,128)(2,1)}, bf16[4,256,512]{2,1,0:T(8,128)(2,1)}, u32[]{:S(2)}, u32[]{:S(2)}) collective-permute-start(bf16[4,256,512]{2,1,0:T(8,128)(2,1)} %get-tuple-element.134), channel_id=1, source_target_pairs={{0,1},{1,2},{2,3},{4,5},{5,6},{6,7},{8,9},{9,10},{10,11},{12,13},{... | collective-permute-start | bytes 3145736 | tf_op jit(solution)/shard_map/ppermute | solution.py:787
  263.2 37.1 %collective-permute-start.26 = (bf16[4,256,512]{2,1,0:T(8,128)(2,1)}, bf16[4,256,512]{2,1,0:T(8,128)(2,1)}, u32[]{:S(2)}, u32[]{:S(2)}) collective-permute-start(bf16[4,256,512]{2,1,0:T(8,128)(2,1)} %get-tuple-element.135), channel_id=1, source_target_pairs={{1,0},{2,1},{3,2},{5,4},{6,5},{7,6},{9,8},{10,9},{11,10},{13,12},{... | collective-permute-start | bytes 3145736 | tf_op jit(solution)/shard_map/ppermute | solution.py:786
  314.4 28.9 %collective-permute-start.54 = (bf16[1,3968,128]{2,1,0:T(8,128)(2,1)S(1)}, bf16[1,3968,128]{2,1,0:T(8,128)(2,1)S(1)}, u32[]{:S(2)}, u32[]{:S(2)}) collective-permute-start(bf16[1,3968,128]{2,1,0:T(8,128)(2,1)S(1)} %fusion.2), channel_id=1, source_target_pairs={{0,4},{4,0},{8,12},{12,8},{16,20},{20,16},{24,28},{28,24},{1,5},{5... | collective-permute-start | bytes 3047432 | tf_op jit(solution)/shard_map/ppermute | solution.py:504
  316.9 21.0 %collective-permute-start.48 = (bf16[1,144,128]{2,1,0:T(8,128)(2,1)S(1)}, bf16[1,144,128]{2,1,0:T(8,128)(2,1)S(1)}, u32[]{:S(2)}, u32[]{:S(2)}) collective-permute-start(bf16[1,144,128]{2,1,0:T(8,128)(2,1)S(1)} %fusion.17), channel_id=1, source_target_pairs={{0,4},{4,0},{8,12},{12,8},{16,20},{20,16},{24,28},{28,24},{1,5},{5... | collective-permute-start | bytes 110600 | tf_op jit(solution)/shard_map/ppermute | solution.py:504
  338.7 39.4 %collective-permute-start.28 = (bf16[4,1152,128]{2,1,0:T(8,128)(2,1)S(1)}, bf16[4,1152,128]{2,1,0:T(8,128)(2,1)S(1)}, u32[]{:S(2)}, u32[]{:S(2)}) collective-permute-start(bf16[4,1152,128]{2,1,0:T(8,128)(2,1)S(1)} %dynamic-slice_bitcast_fusion.2), channel_id=1, source_target_pairs={{0,2},{1,3},{2,0},{3,1},{4,6},{5,7},{6,4},{7,5},{8,10},{9,11},{10,... | collective-permute-start | bytes 3538952 | tf_op jit(solution)/shard_map/ppermute | solution.py:504
  352.7 23.0 %collective-permute-start.55 = (bf16[1,1984,128]{2,1,0:T(8,128)(2,1)S(1)}, bf16[1,1984,128]{2,1,0:T(8,128)(2,1)S(1)}, u32[]{:S(2)}, u32[]{:S(2)}) collective-permute-start(bf16[1,1984,128]{2,1,0:T(8,128)(2,1)S(1)} %fusion.5), channel_id=1, source_target_pairs={{0,2},{1,3},{2,0},{3,1},{4,6},{5,7},{6,4},{7,5},{8,10},{9,11},{10,... | collective-permute-start | bytes 1523720 | tf_op jit(solution)/shard_map/ppermute | solution.py:504
  353.4 33.3 %collective-permute-start.36 = (bf16[4,1152,128]{2,1,0:T(8,128)(2,1)S(1)}, bf16[4,1152,128]{2,1,0:T(8,128)(2,1)S(1)}, u32[]{:S(2)}, u32[]{:S(2)}) collective-permute-start(bf16[4,1152,128]{2,1,0:T(8,128)(2,1)S(1)} %dynamic-slice_bitcast_fusion.1), channel_id=1, source_target_pairs={{0,4},{4,0},{8,12},{12,8},{16,20},{20,16},{24,28},{28,24},{1,5},{5... | collective-permute-start | bytes 3538952 | tf_op jit(solution)/shard_map/ppermute | solution.py:504
  378.4 23.3 %collective-permute-start.29 = (bf16[4,576,128]{2,1,0:T(8,128)(2,1)S(1)}, bf16[4,576,128]{2,1,0:T(8,128)(2,1)S(1)}, u32[]{:S(2)}, u32[]{:S(2)}) collective-permute-start(bf16[4,576,128]{2,1,0:T(8,128)(2,1)S(1)} %fusion.3), channel_id=1, source_target_pairs={{0,4},{4,0},{8,12},{12,8},{16,20},{20,16},{24,28},{28,24},{1,5},{5... | collective-permute-start | bytes 1769480 | tf_op jit(solution)/shard_map/ppermute | solution.py:504
  404.5 15.7 %collective-permute-start.38 = (bf16[4,288,128]{2,1,0:T(8,128)(2,1)S(1)}, bf16[4,288,128]{2,1,0:T(8,128)(2,1)S(1)}, u32[]{:S(2)}, u32[]{:S(2)}) collective-permute-start(bf16[4,288,128]{2,1,0:T(8,128)(2,1)S(1)} %fusion.7), channel_id=1, source_target_pairs={{0,8},{4,12},{8,0},{12,4},{16,24},{20,28},{24,16},{28,20},{1,9},{5... | collective-permute-start | bytes 884744 | tf_op jit(solution)/shard_map/ppermute | solution.py:504
  411.3 28.4 %collective-permute-start.60 = (bf16[1,1984,128]{2,1,0:T(8,128)(2,1)S(1)}, bf16[1,1984,128]{2,1,0:T(8,128)(2,1)S(1)}, u32[]{:S(2)}, u32[]{:S(2)}) collective-permute-start(bf16[1,1984,128]{2,1,0:T(8,128)(2,1)S(1)} %pad_maximum_fusion.8), channel_id=1, source_target_pairs={{0,2},{1,3},{2,0},{3,1},{4,6},{5,7},{6,4},{7,5},{8,10},{9,11},{10,... | collective-permute-start | bytes 1523720 | tf_op jit(solution)/shard_map/ppermute | solution.py:504
  413.7 14.6 %collective-permute-start.31 = (bf16[4,144,128]{2,1,0:T(8,128)(2,1)S(1)}, bf16[4,144,128]{2,1,0:T(8,128)(2,1)S(1)}, u32[]{:S(2)}, u32[]{:S(2)}) collective-permute-start(bf16[4,144,128]{2,1,0:T(8,128)(2,1)S(1)} %fusion.13), channel_id=1, source_target_pairs={{0,16},{4,20},{8,24},{12,28},{16,0},{20,4},{24,8},{28,12},{1,17},{... | collective-permute-start | bytes 442376 | tf_op jit(solution)/shard_map/ppermute | solution.py:504
  443.4 16.3 %collective-permute-start.34 = (bf16[4,576,128]{2,1,0:T(8,128)(2,1)S(1)}, bf16[4,576,128]{2,1,0:T(8,128)(2,1)S(1)}, u32[]{:S(2)}, u32[]{:S(2)}) collective-permute-start(bf16[4,576,128]{2,1,0:T(8,128)(2,1)S(1)} %pad_maximum_fusion.6), channel_id=1, source_target_pairs={{0,4},{4,0},{8,12},{12,8},{16,20},{20,16},{24,28},{28,24},{1,5},{5... | collective-permute-start | bytes 1769480 | tf_op jit(solution)/shard_map/ppermute | solution.py:504
  446.5 16.3 %collective-permute-start.42 = (bf16[4,576,128]{2,1,0:T(8,128)(2,1)S(1)}, bf16[4,576,128]{2,1,0:T(8,128)(2,1)S(1)}, u32[]{:S(2)}, u32[]{:S(2)}) collective-permute-start(bf16[4,576,128]{2,1,0:T(8,128)(2,1)S(1)} %pad_maximum_fusion.7), channel_id=1, source_target_pairs={{0,2},{1,3},{2,0},{3,1},{4,6},{5,7},{6,4},{7,5},{8,10},{9,11},{10,... | collective-permute-start | bytes 1769480 | tf_op jit(solution)/shard_map/ppermute | solution.py:504
  448.0 33.5 %collective-permute-start.61 = (bf16[1,3968,128]{2,1,0:T(8,128)(2,1)S(1)}, bf16[1,3968,128]{2,1,0:T(8,128)(2,1)S(1)}, u32[]{:S(2)}, u32[]{:S(2)}) collective-permute-start(bf16[1,3968,128]{2,1,0:T(8,128)(2,1)S(1)} %pad_maximum_fusion.5), channel_id=1, source_target_pairs={{0,4},{4,0},{8,12},{12,8},{16,20},{20,16},{24,28},{28,24},{1,5},{5... | collective-permute-start | bytes 3047432 | tf_op jit(solution)/shard_map/ppermute | solution.py:504
  460.0 22.1 %collective-permute-start.35 = (bf16[4,1152,128]{2,1,0:T(8,128)(2,1)S(1)}, bf16[4,1152,128]{2,1,0:T(8,128)(2,1)S(1)}, u32[]{:S(2)}, u32[]{:S(2)}) collective-permute-start(bf16[4,1152,128]{2,1,0:T(8,128)(2,1)S(1)} %pad_maximum_fusion.3), channel_id=1, source_target_pairs={{0,2},{1,3},{2,0},{3,1},{4,6},{5,7},{6,4},{7,5},{8,10},{9,11},{10,... | collective-permute-start | bytes 3538952 | tf_op jit(solution)/shard_map/ppermute | solution.py:504
  463.2 34.8 %collective-permute-start.43 = (bf16[4,1152,128]{2,1,0:T(8,128)(2,1)S(1)}, bf16[4,1152,128]{2,1,0:T(8,128)(2,1)S(1)}, u32[]{:S(2)}, u32[]{:S(2)}) collective-permute-start(bf16[4,1152,128]{2,1,0:T(8,128)(2,1)S(1)} %pad_maximum_fusion.4), channel_id=1, source_target_pairs={{0,4},{4,0},{8,12},{12,8},{16,20},{20,16},{24,28},{28,24},{1,5},{5... | collective-permute-start | bytes 3538952 | tf_op jit(solution)/shard_map/ppermute | solution.py:504
  482.0 31.3 %collective-permute-start.62 = (bf16[1,7936,128]{2,1,0:T(8,128)(2,1)S(1)}, bf16[1,7936,128]{2,1,0:T(8,128)(2,1)S(1)}, u32[]{:S(2)}, u32[]{:S(2)}) collective-permute-start(bf16[1,7936,128]{2,1,0:T(8,128)(2,1)S(1)} %pad_maximum_fusion.2), channel_id=1, source_target_pairs={{0,1},{1,0},{2,3},{3,2},{4,5},{5,4},{6,7},{7,6},{8,9},{9,8},{10,11... | collective-permute-start | bytes 6094856 | tf_op jit(solution)/shard_map/ppermute | solution.py:504
  509.2 36.3 %collective-permute-start.52 = (bf16[9,2304,128]{2,1,0:T(8,128)(2,1)}, bf16[9,2304,128]{2,1,0:T(8,128)(2,1)}, u32[]{:S(2)}, u32[]{:S(2)}) collective-permute-start(bf16[9,2304,128]{2,1,0:T(8,128)(2,1)} %maximum_maximum_fusion.own), channel_id=1, source_target_pairs={{0,1},{1,0},{2,3},{3,2},{4,5},{5,4},{6,7},{7,6},{8,9},{9,8},{10,11... | collective-permute-start | bytes 15925256 | tf_op jit(solution)/shard_map/ppermute | solution.py:504
  (96 other events, 1057.5 us)
